TPU v7x, 32 devices: a whole 2x2x4 slice. The times are simulated.
32 devices in a mesh: blk: 8 (over z, y), group: 4 (over x, core).
Axes of the slice: x: 2, y: 2, z: 4, core: 2. Of those that a mesh axis runs over, the one named last changes fastest.
Arguments:
- image_embeds: bfloat16 [4, 768, 1152], P('group', 'blk')
- text_embeds: bfloat16 [4, 768, 1152], P('group', 'blk'), may hold values from -0.1875 to 0.1875
- positives: int32 [4, 768], P('group', 'blk'), may hold values from 0 to 767, each once within a row
- partner: int32 [4], replicated, may hold values from 0 to 3, each once
- log_temp: float32 [1], replicated, may hold values from 1.6 to 2.4
- bias: float32 [1], replicated, may hold values from -4 to -2
Outputs:
- image_grads: float32 [4, 768, 1152], P('group', 'blk')
- text_grads: float32 [4, 768, 1152], P('group', 'blk')
- loss: float32 [1], replicated
Inputs may be any that keep to these rules, and one draw needn't show every extreme that they name: Each group's positives name every text row of its partner group exactly once. `partner`: every group is named exactly once.
All inputs are finite; a program needn't handle non-finite values.
Results may differ from a plain program's by a relative error of at most 0.0015.
Values may be sent and summed in bfloat16 or wider, within the bound.
No kernel may reach another device: no remote copies, remote signals or barrier semaphores. Data moves between devices by JAX's collectives and lax.ppermute only.
A program may use at most 64 MiB of HBM per device.

v0:
```python
import jax
import jax.numpy as jnp
from jax import lax
from jax.sharding import PartitionSpec as P


def shifted(array, axis, by):
    size = lax.axis_size(axis)
    return lax.ppermute(array, axis, [(i, (i + by) % size) for i in range(size)])


def pair_block(images, texts, hits, temper, offset):
    logits = temper * jnp.dot(images, texts.T, preferred_element_type=jnp.float32) + offset
    hit_values = hits.astype(jnp.float32)
    losses = jax.nn.softplus(logits) - hit_values * logits
    slopes = (jax.nn.sigmoid(logits) - hit_values).astype(jnp.bfloat16)
    return (jnp.sum(losses), slopes)


def shards(image_embeds, text_embeds, positives, partner, log_temp, bias):
    temper = jnp.exp(log_temp[0])
    offset = bias[0]
    images = image_embeds[0]
    own_texts = text_embeds[0]
    own_labels = positives[0]
    rows = images.shape[0]
    width = images.shape[1]
    cycle_size = lax.axis_size("blk")
    group_count = lax.axis_size("group")
    blk_place = lax.axis_index("blk")
    group_place = lax.axis_index("group")
    every_text = lax.all_gather(own_texts, "group", axis=0, tiled=True)
    target = partner[group_place]
    partner_block = lax.dynamic_slice_in_dim(every_text, target * rows, rows, 0)
    columns = jnp.arange(rows, dtype=jnp.int32)

    def hits_for(labels, source):
        return labels[:, None] == (source * rows + columns)[None, :]

    def work(visit_images, visit_texts, visit_labels, source, image_sum, text_sum, total):
        part, slopes = pair_block(images, visit_texts, hits_for(own_labels, source), temper, offset)
        image_sum = image_sum + temper * jnp.dot(
            slopes, visit_texts, preferred_element_type=jnp.float32
        )
        unused, back_slopes = pair_block(
            visit_images, partner_block, hits_for(visit_labels, blk_place), temper, offset
        )
        text_sum = text_sum + temper * jnp.dot(
            back_slopes.T, visit_images, preferred_element_type=jnp.float32
        )
        return (image_sum, text_sum, total + part)

    zero_block = jnp.zeros((rows, width), jnp.float32)
    zero_total = jnp.zeros((), jnp.float32)

    def advance(step, carry):
        visit_images, visit_texts, visit_labels, image_sum, text_sum, total = carry
        source = (blk_place - step) % cycle_size
        image_sum, text_sum, total = work(
            visit_images, visit_texts, visit_labels, source, image_sum, text_sum, total
        )
        visit_images, visit_texts = shifted((visit_images, visit_texts), "blk", 1)
        visit_labels = shifted(visit_labels, "blk", 1)
        return (visit_images, visit_texts, visit_labels, image_sum, text_sum, total)

    start = (images, partner_block, own_labels, zero_block, zero_block, zero_total)
    finished = lax.fori_loop(0, cycle_size, advance, start)
    image_sum = finished[3]
    text_sum = finished[4]
    total = finished[5]
    spread = jnp.zeros((group_count * rows, width), jnp.float32)
    spread = lax.dynamic_update_slice_in_dim(spread, text_sum, target * rows, 0)
    text_home = lax.psum_scatter(spread, "group", scatter_dimension=0, tiled=True)
    total = lax.psum(total, ("blk", "group"))
    loss = total / (group_count * rows * cycle_size * cycle_size)
    return (image_sum[None], text_home[None], jnp.reshape(loss, (1,)))


def solution(mesh):
    in_specs = (P("group", "blk", None), P("group", "blk", None), P("group", "blk"), P(), P(), P())
    out_specs = (P("group", "blk", None), P("group", "blk", None), P())
    return jax.shard_map(shards, mesh=mesh, in_specs=in_specs, out_specs=out_specs, check_vma=False)
```

profile of v0, /device:TPU:0, one launch (start us, length us, event | category | flops | bytes accessed | tf_op | source)
XLA Modules:
  0.0 173.0 jit_solution(16592030936822947731)
XLA Ops:
  8.0 1.2 dynamic_slice.6
  11.5 10.8 %all-gather = bf16[1,384,1152]{2,1,0:T(8,128)(2,1)S(1)} all-gather(bf16[1,96,1152]{2,1,0:T(8,128)(2,1)} %param.9), channel_id=2, replica_groups=mesh['blk'=8,'group'=4] {'group'}, dimensions={1}, use_global_device_ids=true | all-gather | bytes 1105920 | tf_op jit(solution)/shard_map/all_gather | solution.py:32
  22.3 102.0 %while.27 = (s32[]{:T(128)}, bf16[96,1152]{1,0:T(8,128)(2,1)S(1)}, bf16[96,1152]{1,0:T(8,128)(2,1)S(1)}, s32[96]{0:T(128)S(1)}, f32[96,1152]{1,0:T(8,128)S(1)}, ...) while((s32[]{:T(128)}, bf16[96,1152]{1,0:T(8,128)(2,1)S(1)}, ...), condition=%wide.region_2.3_spmd.clone.clone, body=%wide.region_0.2_spmd.clone.clone.sunk | while | flops 85856464 | bytes 5609185 | solution.py:67
  22.3 1.6 collective-permute-start.2
  23.9 1.6 collective-permute-start
  25.5 1.6 collective-permute-start.1
  27.1 1.5 fusion.52
  28.6 1.3 fusion.54
  30.8 4.2 %collective-permute-done = bf16[96,1152]{1,0:T(8,128)(2,1)S(1)} collective-permute-done((bf16[96,1152]{1,0:T(8,128)(2,1)S(1)}, bf16[96,1152]{1,0:T(8,128)(2,1)S(1)}, u32[]{:S(2)}, u32[]{:S(2)}) %collective-permute-start) | collective-permute-done | bytes 221216 | tf_op jit(solution)/shard_map/while/body/eval_jaxpr/ppermute | solution.py:9
  35.0 3.9 %collective-permute-done.1 = bf16[96,1152]{1,0:T(8,128)(2,1)S(1)} collective-permute-done((bf16[96,1152]{1,0:T(8,128)(2,1)S(1)}, bf16[96,1152]{1,0:T(8,128)(2,1)S(1)}, u32[]{:S(2)}, u32[]{:S(2)}) %collective-permute-start.1) | collective-permute-done | bytes 221216 | tf_op jit(solution)/shard_map/while/body/eval_jaxpr/ppermute | solution.py:9
  38.9 1.3 collective-permute-start
  40.9 1.5 fusion.52
  42.4 1.3 fusion.54
  45.1 4.8 %collective-permute-done = bf16[96,1152]{1,0:T(8,128)(2,1)S(1)} collective-permute-done((bf16[96,1152]{1,0:T(8,128)(2,1)S(1)}, bf16[96,1152]{1,0:T(8,128)(2,1)S(1)}, u32[]{:S(2)}, u32[]{:S(2)}) %collective-permute-start) | collective-permute-done | bytes 221216 | tf_op jit(solution)/shard_map/while/body/eval_jaxpr/ppermute | solution.py:9
  50.0 2.9 %collective-permute-done.1 = bf16[96,1152]{1,0:T(8,128)(2,1)S(1)} collective-permute-done((bf16[96,1152]{1,0:T(8,128)(2,1)S(1)}, bf16[96,1152]{1,0:T(8,128)(2,1)S(1)}, u32[]{:S(2)}, u32[]{:S(2)}) %collective-permute-start.1) | collective-permute-done | bytes 221216 | tf_op jit(solution)/shard_map/while/body/eval_jaxpr/ppermute | solution.py:9
  53.0 1.3 collective-permute-start.1
  54.4 1.5 fusion.52
  55.9 1.3 fusion.54
  58.1 1.2 collective-permute-done.2
  59.2 4.5 %collective-permute-done = bf16[96,1152]{1,0:T(8,128)(2,1)S(1)} collective-permute-done((bf16[96,1152]{1,0:T(8,128)(2,1)S(1)}, bf16[96,1152]{1,0:T(8,128)(2,1)S(1)}, u32[]{:S(2)}, u32[]{:S(2)}) %collective-permute-start) | collective-permute-done | bytes 221216 | tf_op jit(solution)/shard_map/while/body/eval_jaxpr/ppermute | solution.py:9
  63.7 2.4 %collective-permute-done.1 = bf16[96,1152]{1,0:T(8,128)(2,1)S(1)} collective-permute-done((bf16[96,1152]{1,0:T(8,128)(2,1)S(1)}, bf16[96,1152]{1,0:T(8,128)(2,1)S(1)}, u32[]{:S(2)}, u32[]{:S(2)}) %collective-permute-start.1) | collective-permute-done | bytes 221216 | tf_op jit(solution)/shard_map/while/body/eval_jaxpr/ppermute | solution.py:9
  66.3 1.5 fusion.52
  67.8 1.3 fusion.54
  70.0 2.4 %collective-permute-done.2 = s32[96]{0:T(128)S(1)} collective-permute-done((s32[96]{0:T(128)S(1)}, s32[96]{0:T(128)S(1)}, u32[]{:S(2)}, u32[]{:S(2)}) %collective-permute-start.2) | collective-permute-done | bytes 416 | tf_op jit(solution)/shard_map/while/body/eval_jaxpr/ppermute | solution.py:9
  72.4 3.6 %collective-permute-done = bf16[96,1152]{1,0:T(8,128)(2,1)S(1)} collective-permute-done((bf16[96,1152]{1,0:T(8,128)(2,1)S(1)}, bf16[96,1152]{1,0:T(8,128)(2,1)S(1)}, u32[]{:S(2)}, u32[]{:S(2)}) %collective-permute-start) | collective-permute-done | bytes 221216 | tf_op jit(solution)/shard_map/while/body/eval_jaxpr/ppermute | solution.py:9
  76.0 2.4 %collective-permute-done.1 = bf16[96,1152]{1,0:T(8,128)(2,1)S(1)} collective-permute-done((bf16[96,1152]{1,0:T(8,128)(2,1)S(1)}, bf16[96,1152]{1,0:T(8,128)(2,1)S(1)}, u32[]{:S(2)}, u32[]{:S(2)}) %collective-permute-start.1) | collective-permute-done | bytes 221216 | tf_op jit(solution)/shard_map/while/body/eval_jaxpr/ppermute | solution.py:9
  78.6 1.5 fusion.52
  80.1 1.3 fusion.54
  82.3 2.4 %collective-permute-done.2 = s32[96]{0:T(128)S(1)} collective-permute-done((s32[96]{0:T(128)S(1)}, s32[96]{0:T(128)S(1)}, u32[]{:S(2)}, u32[]{:S(2)}) %collective-permute-start.2) | collective-permute-done | bytes 416 | tf_op jit(solution)/shard_map/while/body/eval_jaxpr/ppermute | solution.py:9
  84.7 2.7 %collective-permute-done = bf16[96,1152]{1,0:T(8,128)(2,1)S(1)} collective-permute-done((bf16[96,1152]{1,0:T(8,128)(2,1)S(1)}, bf16[96,1152]{1,0:T(8,128)(2,1)S(1)}, u32[]{:S(2)}, u32[]{:S(2)}) %collective-permute-start) | collective-permute-done | bytes 221216 | tf_op jit(solution)/shard_map/while/body/eval_jaxpr/ppermute | solution.py:9
  87.3 2.4 %collective-permute-done.1 = bf16[96,1152]{1,0:T(8,128)(2,1)S(1)} collective-permute-done((bf16[96,1152]{1,0:T(8,128)(2,1)S(1)}, bf16[96,1152]{1,0:T(8,128)(2,1)S(1)}, u32[]{:S(2)}, u32[]{:S(2)}) %collective-permute-start.1) | collective-permute-done | bytes 221216 | tf_op jit(solution)/shard_map/while/body/eval_jaxpr/ppermute | solution.py:9
  89.9 1.5 fusion.52
  91.4 1.3 fusion.54
  93.6 2.3 %collective-permute-done.2 = s32[96]{0:T(128)S(1)} collective-permute-done((s32[96]{0:T(128)S(1)}, s32[96]{0:T(128)S(1)}, u32[]{:S(2)}, u32[]{:S(2)}) %collective-permute-start.2) | collective-permute-done | bytes 416 | tf_op jit(solution)/shard_map/while/body/eval_jaxpr/ppermute | solution.py:9
  95.9 2.5 %collective-permute-done = bf16[96,1152]{1,0:T(8,128)(2,1)S(1)} collective-permute-done((bf16[96,1152]{1,0:T(8,128)(2,1)S(1)}, bf16[96,1152]{1,0:T(8,128)(2,1)S(1)}, u32[]{:S(2)}, u32[]{:S(2)}) %collective-permute-start) | collective-permute-done | bytes 221216 | tf_op jit(solution)/shard_map/while/body/eval_jaxpr/ppermute | solution.py:9
  98.4 2.5 %collective-permute-done.1 = bf16[96,1152]{1,0:T(8,128)(2,1)S(1)} collective-permute-done((bf16[96,1152]{1,0:T(8,128)(2,1)S(1)}, bf16[96,1152]{1,0:T(8,128)(2,1)S(1)}, u32[]{:S(2)}, u32[]{:S(2)}) %collective-permute-start.1) | collective-permute-done | bytes 221216 | tf_op jit(solution)/shard_map/while/body/eval_jaxpr/ppermute | solution.py:9
  101.2 1.5 fusion.52
  102.7 1.3 fusion.54
  104.9 2.3 %collective-permute-done.2 = s32[96]{0:T(128)S(1)} collective-permute-done((s32[96]{0:T(128)S(1)}, s32[96]{0:T(128)S(1)}, u32[]{:S(2)}, u32[]{:S(2)}) %collective-permute-start.2) | collective-permute-done | bytes 416 | tf_op jit(solution)/shard_map/while/body/eval_jaxpr/ppermute | solution.py:9
  107.2 2.5 %collective-permute-done = bf16[96,1152]{1,0:T(8,128)(2,1)S(1)} collective-permute-done((bf16[96,1152]{1,0:T(8,128)(2,1)S(1)}, bf16[96,1152]{1,0:T(8,128)(2,1)S(1)}, u32[]{:S(2)}, u32[]{:S(2)}) %collective-permute-start) | collective-permute-done | bytes 221216 | tf_op jit(solution)/shard_map/while/body/eval_jaxpr/ppermute | solution.py:9
  109.6 3.6 %collective-permute-done.1 = bf16[96,1152]{1,0:T(8,128)(2,1)S(1)} collective-permute-done((bf16[96,1152]{1,0:T(8,128)(2,1)S(1)}, bf16[96,1152]{1,0:T(8,128)(2,1)S(1)}, u32[]{:S(2)}, u32[]{:S(2)}) %collective-permute-start.1) | collective-permute-done | bytes 221216 | tf_op jit(solution)/shard_map/while/body/eval_jaxpr/ppermute | solution.py:9
  113.5 1.3 collective-permute-start.1
  114.8 1.5 fusion.52
  116.3 1.2 fusion.54
  119.5 2.5 %collective-permute-done = bf16[96,1152]{1,0:T(8,128)(2,1)S(1)} collective-permute-done((bf16[96,1152]{1,0:T(8,128)(2,1)S(1)}, bf16[96,1152]{1,0:T(8,128)(2,1)S(1)}, u32[]{:S(2)}, u32[]{:S(2)}) %collective-permute-start) | collective-permute-done | bytes 221216 | tf_op jit(solution)/shard_map/while/body/eval_jaxpr/ppermute | solution.py:9
  122.0 2.4 %collective-permute-done.1 = bf16[96,1152]{1,0:T(8,128)(2,1)S(1)} collective-permute-done((bf16[96,1152]{1,0:T(8,128)(2,1)S(1)}, bf16[96,1152]{1,0:T(8,128)(2,1)S(1)}, u32[]{:S(2)}, u32[]{:S(2)}) %collective-permute-start.1) | collective-permute-done | bytes 221216 | tf_op jit(solution)/shard_map/while/body/eval_jaxpr/ppermute | solution.py:9
  124.5 1.2 copy-done.1
  125.8 38.6 %psum.7 = f32[]{:T(128)} all-reduce(f32[]{:T(128)} %get-tuple-element.347), channel_id=1, replica_groups=mesh['blk'=8,'group'=4] {'blk','group'}, use_global_device_ids=true, to_apply=%region_4.5 | all-reduce | flops 1 | bytes 8 | tf_op jit(solution)/shard_map/psum | solution.py:74
  (87 shorter events, 7.6 us)
Async XLA Ops:
  7.2 15.1 %copy-start.3 = (s32[1,96]{1,0:T(1,128)S(1)}, s32[1,96]{1,0:T(1,128)}, u32[]{:S(2)}) copy-start(s32[1,96]{1,0:T(1,128)} %param.10) | copy-start | bytes 1156
  7.2 15.1 %copy-start.2 = (bf16[1,96,1152]{2,1,0:T(8,128)(2,1)S(1)}, bf16[1,96,1152]{2,1,0:T(8,128)(2,1)}, u32[]{:S(2)}) copy-start(bf16[1,96,1152]{2,1,0:T(8,128)(2,1)} %param.8) | copy-start | bytes 663556
  7.2 157.9 %reduce-scatter.2.cloned.1.call-start = ((), (), s32[]{:S(2)}) async-start(), calls=%async_computation.1 | async-start | bytes 2211840 | tf_op jit(solution)/shard_map/reduce_scatter | solution.py:73
  22.3 8.5 %collective-permute-start.2 = (s32[96]{0:T(128)S(1)}, s32[96]{0:T(128)S(1)}, u32[]{:S(2)}, u32[]{:S(2)}) collective-permute-start(s32[96]{0:T(128)S(1)} %copy.19), channel_id=1, source_target_pairs={{0,4},{4,8},{8,12},{12,16},{16,20},{20,24},{24,28},{28,0},{1,5},{5... | collective-permute-start | bytes 1160 | tf_op jit(solution)/shard_map/while/body/eval_jaxpr/ppermute | solution.py:9
  23.9 11.0 %collective-permute-start = (bf16[96,1152]{1,0:T(8,128)(2,1)S(1)}, bf16[96,1152]{1,0:T(8,128)(2,1)S(1)}, u32[]{:S(2)}, u32[]{:S(2)}) collective-permute-start(bf16[96,1152]{1,0:T(8,128)(2,1)S(1)} %copy.17), channel_id=1, source_target_pairs={{0,4},{4,8},{8,12},{12,16},{16,20},{20,24},{24,28},{28,0},{1,5},{5... | collective-permute-start | bytes 663560 | tf_op jit(solution)/shard_map/while/body/eval_jaxpr/ppermute | solution.py:9
  25.5 13.3 %collective-permute-start.1 = (bf16[96,1152]{1,0:T(8,128)(2,1)S(1)}, bf16[96,1152]{1,0:T(8,128)(2,1)S(1)}, u32[]{:S(2)}, u32[]{:S(2)}) collective-permute-start(bf16[96,1152]{1,0:T(8,128)(2,1)S(1)} %copy.18), channel_id=1, source_target_pairs={{0,4},{4,8},{8,12},{12,16},{16,20},{20,24},{24,28},{28,0},{1,5},{5... | collective-permute-start | bytes 663560 | tf_op jit(solution)/shard_map/while/body/eval_jaxpr/ppermute | solution.py:9
  38.8 6.3 %collective-permute-start.2 = (s32[96]{0:T(128)S(1)}, s32[96]{0:T(128)S(1)}, u32[]{:S(2)}, u32[]{:S(2)}) collective-permute-start(s32[96]{0:T(128)S(1)} %copy.19), channel_id=1, source_target_pairs={{0,4},{4,8},{8,12},{12,16},{16,20},{20,24},{24,28},{28,0},{1,5},{5... | collective-permute-start | bytes 1160 | tf_op jit(solution)/shard_map/while/body/eval_jaxpr/ppermute | solution.py:9
  38.9 11.1 %collective-permute-start = (bf16[96,1152]{1,0:T(8,128)(2,1)S(1)}, bf16[96,1152]{1,0:T(8,128)(2,1)S(1)}, u32[]{:S(2)}, u32[]{:S(2)}) collective-permute-start(bf16[96,1152]{1,0:T(8,128)(2,1)S(1)} %copy.17), channel_id=1, source_target_pairs={{0,4},{4,8},{8,12},{12,16},{16,20},{20,24},{24,28},{28,0},{1,5},{5... | collective-permute-start | bytes 663560 | tf_op jit(solution)/shard_map/while/body/eval_jaxpr/ppermute | solution.py:9
  40.2 12.8 %collective-permute-start.1 = (bf16[96,1152]{1,0:T(8,128)(2,1)S(1)}, bf16[96,1152]{1,0:T(8,128)(2,1)S(1)}, u32[]{:S(2)}, u32[]{:S(2)}) collective-permute-start(bf16[96,1152]{1,0:T(8,128)(2,1)S(1)} %copy.18), channel_id=1, source_target_pairs={{0,4},{4,8},{8,12},{12,16},{16,20},{20,24},{24,28},{28,0},{1,5},{5... | collective-permute-start | bytes 663560 | tf_op jit(solution)/shard_map/while/body/eval_jaxpr/ppermute | solution.py:9
  52.9 6.3 %collective-permute-start.2 = (s32[96]{0:T(128)S(1)}, s32[96]{0:T(128)S(1)}, u32[]{:S(2)}, u32[]{:S(2)}) collective-permute-start(s32[96]{0:T(128)S(1)} %copy.19), channel_id=1, source_target_pairs={{0,4},{4,8},{8,12},{12,16},{16,20},{20,24},{24,28},{28,0},{1,5},{5... | collective-permute-start | bytes 1160 | tf_op jit(solution)/shard_map/while/body/eval_jaxpr/ppermute | solution.py:9
  52.9 10.8 %collective-permute-start = (bf16[96,1152]{1,0:T(8,128)(2,1)S(1)}, bf16[96,1152]{1,0:T(8,128)(2,1)S(1)}, u32[]{:S(2)}, u32[]{:S(2)}) collective-permute-start(bf16[96,1152]{1,0:T(8,128)(2,1)S(1)} %copy.17), channel_id=1, source_target_pairs={{0,4},{4,8},{8,12},{12,16},{16,20},{20,24},{24,28},{28,0},{1,5},{5... | collective-permute-start | bytes 663560 | tf_op jit(solution)/shard_map/while/body/eval_jaxpr/ppermute | solution.py:9
  53.0 13.1 %collective-permute-start.1 = (bf16[96,1152]{1,0:T(8,128)(2,1)S(1)}, bf16[96,1152]{1,0:T(8,128)(2,1)S(1)}, u32[]{:S(2)}, u32[]{:S(2)}) collective-permute-start(bf16[96,1152]{1,0:T(8,128)(2,1)S(1)} %copy.18), channel_id=1, source_target_pairs={{0,4},{4,8},{8,12},{12,16},{16,20},{20,24},{24,28},{28,0},{1,5},{5... | collective-permute-start | bytes 663560 | tf_op jit(solution)/shard_map/while/body/eval_jaxpr/ppermute | solution.py:9
  66.1 6.3 %collective-permute-start.2 = (s32[96]{0:T(128)S(1)}, s32[96]{0:T(128)S(1)}, u32[]{:S(2)}, u32[]{:S(2)}) collective-permute-start(s32[96]{0:T(128)S(1)} %copy.19), channel_id=1, source_target_pairs={{0,4},{4,8},{8,12},{12,16},{16,20},{20,24},{24,28},{28,0},{1,5},{5... | collective-permute-start | bytes 1160 | tf_op jit(solution)/shard_map/while/body/eval_jaxpr/ppermute | solution.py:9
  66.1 9.9 %collective-permute-start = (bf16[96,1152]{1,0:T(8,128)(2,1)S(1)}, bf16[96,1152]{1,0:T(8,128)(2,1)S(1)}, u32[]{:S(2)}, u32[]{:S(2)}) collective-permute-start(bf16[96,1152]{1,0:T(8,128)(2,1)S(1)} %copy.17), channel_id=1, source_target_pairs={{0,4},{4,8},{8,12},{12,16},{16,20},{20,24},{24,28},{28,0},{1,5},{5... | collective-permute-start | bytes 663560 | tf_op jit(solution)/shard_map/while/body/eval_jaxpr/ppermute | solution.py:9
  66.2 12.1 %collective-permute-start.1 = (bf16[96,1152]{1,0:T(8,128)(2,1)S(1)}, bf16[96,1152]{1,0:T(8,128)(2,1)S(1)}, u32[]{:S(2)}, u32[]{:S(2)}) collective-permute-start(bf16[96,1152]{1,0:T(8,128)(2,1)S(1)} %copy.18), channel_id=1, source_target_pairs={{0,4},{4,8},{8,12},{12,16},{16,20},{20,24},{24,28},{28,0},{1,5},{5... | collective-permute-start | bytes 663560 | tf_op jit(solution)/shard_map/while/body/eval_jaxpr/ppermute | solution.py:9
  78.4 6.3 %collective-permute-start.2 = (s32[96]{0:T(128)S(1)}, s32[96]{0:T(128)S(1)}, u32[]{:S(2)}, u32[]{:S(2)}) collective-permute-start(s32[96]{0:T(128)S(1)} %copy.19), channel_id=1, source_target_pairs={{0,4},{4,8},{8,12},{12,16},{16,20},{20,24},{24,28},{28,0},{1,5},{5... | collective-permute-start | bytes 1160 | tf_op jit(solution)/shard_map/while/body/eval_jaxpr/ppermute | solution.py:9
  78.4 8.9 %collective-permute-start = (bf16[96,1152]{1,0:T(8,128)(2,1)S(1)}, bf16[96,1152]{1,0:T(8,128)(2,1)S(1)}, u32[]{:S(2)}, u32[]{:S(2)}) collective-permute-start(bf16[96,1152]{1,0:T(8,128)(2,1)S(1)} %copy.17), channel_id=1, source_target_pairs={{0,4},{4,8},{8,12},{12,16},{16,20},{20,24},{24,28},{28,0},{1,5},{5... | collective-permute-start | bytes 663560 | tf_op jit(solution)/shard_map/while/body/eval_jaxpr/ppermute | solution.py:9
  78.5 11.2 %collective-permute-start.1 = (bf16[96,1152]{1,0:T(8,128)(2,1)S(1)}, bf16[96,1152]{1,0:T(8,128)(2,1)S(1)}, u32[]{:S(2)}, u32[]{:S(2)}) collective-permute-start(bf16[96,1152]{1,0:T(8,128)(2,1)S(1)} %copy.18), channel_id=1, source_target_pairs={{0,4},{4,8},{8,12},{12,16},{16,20},{20,24},{24,28},{28,0},{1,5},{5... | collective-permute-start | bytes 663560 | tf_op jit(solution)/shard_map/while/body/eval_jaxpr/ppermute | solution.py:9
  89.7 6.2 %collective-permute-start.2 = (s32[96]{0:T(128)S(1)}, s32[96]{0:T(128)S(1)}, u32[]{:S(2)}, u32[]{:S(2)}) collective-permute-start(s32[96]{0:T(128)S(1)} %copy.19), channel_id=1, source_target_pairs={{0,4},{4,8},{8,12},{12,16},{16,20},{20,24},{24,28},{28,0},{1,5},{5... | collective-permute-start | bytes 1160 | tf_op jit(solution)/shard_map/while/body/eval_jaxpr/ppermute | solution.py:9
  89.7 8.7 %collective-permute-start = (bf16[96,1152]{1,0:T(8,128)(2,1)S(1)}, bf16[96,1152]{1,0:T(8,128)(2,1)S(1)}, u32[]{:S(2)}, u32[]{:S(2)}) collective-permute-start(bf16[96,1152]{1,0:T(8,128)(2,1)S(1)} %copy.17), channel_id=1, source_target_pairs={{0,4},{4,8},{8,12},{12,16},{16,20},{20,24},{24,28},{28,0},{1,5},{5... | collective-permute-start | bytes 663560 | tf_op jit(solution)/shard_map/while/body/eval_jaxpr/ppermute | solution.py:9
  89.8 11.1 %collective-permute-start.1 = (bf16[96,1152]{1,0:T(8,128)(2,1)S(1)}, bf16[96,1152]{1,0:T(8,128)(2,1)S(1)}, u32[]{:S(2)}, u32[]{:S(2)}) collective-permute-start(bf16[96,1152]{1,0:T(8,128)(2,1)S(1)} %copy.18), channel_id=1, source_target_pairs={{0,4},{4,8},{8,12},{12,16},{16,20},{20,24},{24,28},{28,0},{1,5},{5... | collective-permute-start | bytes 663560 | tf_op jit(solution)/shard_map/while/body/eval_jaxpr/ppermute | solution.py:9
  100.9 6.2 %collective-permute-start.2 = (s32[96]{0:T(128)S(1)}, s32[96]{0:T(128)S(1)}, u32[]{:S(2)}, u32[]{:S(2)}) collective-permute-start(s32[96]{0:T(128)S(1)} %copy.19), channel_id=1, source_target_pairs={{0,4},{4,8},{8,12},{12,16},{16,20},{20,24},{24,28},{28,0},{1,5},{5... | collective-permute-start | bytes 1160 | tf_op jit(solution)/shard_map/while/body/eval_jaxpr/ppermute | solution.py:9
  101.0 8.7 %collective-permute-start = (bf16[96,1152]{1,0:T(8,128)(2,1)S(1)}, bf16[96,1152]{1,0:T(8,128)(2,1)S(1)}, u32[]{:S(2)}, u32[]{:S(2)}) collective-permute-start(bf16[96,1152]{1,0:T(8,128)(2,1)S(1)} %copy.17), channel_id=1, source_target_pairs={{0,4},{4,8},{8,12},{12,16},{16,20},{20,24},{24,28},{28,0},{1,5},{5... | collective-permute-start | bytes 663560 | tf_op jit(solution)/shard_map/while/body/eval_jaxpr/ppermute | solution.py:9
  101.1 12.2 %collective-permute-start.1 = (bf16[96,1152]{1,0:T(8,128)(2,1)S(1)}, bf16[96,1152]{1,0:T(8,128)(2,1)S(1)}, u32[]{:S(2)}, u32[]{:S(2)}) collective-permute-start(bf16[96,1152]{1,0:T(8,128)(2,1)S(1)} %copy.18), channel_id=1, source_target_pairs={{0,4},{4,8},{8,12},{12,16},{16,20},{20,24},{24,28},{28,0},{1,5},{5... | collective-permute-start | bytes 663560 | tf_op jit(solution)/shard_map/while/body/eval_jaxpr/ppermute | solution.py:9
  113.3 6.2 %collective-permute-start.2 = (s32[96]{0:T(128)S(1)}, s32[96]{0:T(128)S(1)}, u32[]{:S(2)}, u32[]{:S(2)}) collective-permute-start(s32[96]{0:T(128)S(1)} %copy.19), channel_id=1, source_target_pairs={{0,4},{4,8},{8,12},{12,16},{16,20},{20,24},{24,28},{28,0},{1,5},{5... | collective-permute-start | bytes 1160 | tf_op jit(solution)/shard_map/while/body/eval_jaxpr/ppermute | solution.py:9
  113.3 8.7 %collective-permute-start = (bf16[96,1152]{1,0:T(8,128)(2,1)S(1)}, bf16[96,1152]{1,0:T(8,128)(2,1)S(1)}, u32[]{:S(2)}, u32[]{:S(2)}) collective-permute-start(bf16[96,1152]{1,0:T(8,128)(2,1)S(1)} %copy.17), channel_id=1, source_target_pairs={{0,4},{4,8},{8,12},{12,16},{16,20},{20,24},{24,28},{28,0},{1,5},{5... | collective-permute-start | bytes 663560 | tf_op jit(solution)/shard_map/while/body/eval_jaxpr/ppermute | solution.py:9
  113.5 10.8 %collective-permute-start.1 = (bf16[96,1152]{1,0:T(8,128)(2,1)S(1)}, bf16[96,1152]{1,0:T(8,128)(2,1)S(1)}, u32[]{:S(2)}, u32[]{:S(2)}) collective-permute-start(bf16[96,1152]{1,0:T(8,128)(2,1)S(1)} %copy.18), channel_id=1, source_target_pairs={{0,4},{4,8},{8,12},{12,16},{16,20},{20,24},{24,28},{28,0},{1,5},{5... | collective-permute-start | bytes 663560 | tf_op jit(solution)/shard_map/while/body/eval_jaxpr/ppermute | solution.py:9
  124.3 1.4 copy-start
  124.5 1.2 copy-start.1
Sparse Core Ops, SparseCore 0:
  125.9 27.7 reduce-scatter.1
where the time goes:
time: 174 us; the launch traced here: 173 us
  waiting for transfers between devices  61.8 us (36%)
  blocking collectives  49.4 us (28%)
  matrix products  24.4 us (14%)
  between operations  17.3 us (10%)
  starting transfers between devices  10.1 us (6%)
  loops' own time  5.47 us (3%)
  local copies, waits for them, and re-layouts  4.58 us (3%)
    ppermute x24, waiting for transfers between devices, shifted(): lax.ppermute(array, axis, [(i, (i + by) % size) for i in range(size)])  61.7 us
    psum x1, blocking collectives, shards(): total = lax.psum(total, ('blk', 'group'))  38.6 us
    dot_general x8, matrix products, pair_block(): jnp.dot(images, texts.T, preferred_element_type=jnp.float32)  12 us
    all_gather x1, blocking collectives, shards(): every_text = lax.all_gather(own_texts, 'group', axis=0, tiled=True)  10.8 us
    ppermute x24, starting transfers between devices, shifted(): lax.ppermute(array, axis, [(i, (i + by) % size) for i in range(size)])  10 us
    dot_general x8, matrix products, work(): jnp.dot(back_slopes.T, visit_images, preferred_element_type=jnp.float32)  10 us
    another operation x1, loops' own time, shards(): finished = lax.fori_loop(0, cycle_size, advance, start)  5.47 us
  transfers between devices with their start and end apart: 25, of which 23 were waited for; matrix products, arithmetic and copies ran while one was open for 14% of the time, Pallas kernels for 0%

commit v1 on v0

v1 whole, which is shorter than its diff:
```python
import jax
import jax.numpy as jnp
from jax import lax
from jax.sharding import PartitionSpec as P


def pair_slopes(rows, others, hits, temper, offset):
    logits = temper * jnp.dot(rows, others.T, preferred_element_type=jnp.float32) + offset
    hit_values = hits.astype(jnp.float32)
    slopes = (jax.nn.sigmoid(logits) - hit_values).astype(jnp.bfloat16)
    return logits, hit_values, slopes


def shards(image_embeds, text_embeds, positives, partner, log_temp, bias):
    temper = jnp.exp(log_temp[0])
    offset = bias[0]
    images = image_embeds[0]
    texts = text_embeds[0]
    labels = positives[0]
    rows = images.shape[0]
    blocks = lax.axis_size("blk")
    groups = lax.axis_size("group")
    blk_place = lax.axis_index("blk")
    group_place = lax.axis_index("group")
    target = partner[group_place]
    scorer = jnp.argmax(partner == group_place).astype(jnp.int32)

    group_texts = lax.all_gather(texts, "group", axis=0)
    group_images = lax.all_gather(images, "group", axis=0)
    partner_text = lax.dynamic_index_in_dim(group_texts, target, 0, keepdims=False)
    scorer_image = lax.dynamic_index_in_dim(group_images, scorer, 0, keepdims=False)
    all_texts = lax.all_gather(partner_text, "blk", axis=0, tiled=True)
    all_images = lax.all_gather(scorer_image, "blk", axis=0, tiled=True)
    every_label = lax.all_gather(labels, ("blk", "group"), axis=0).reshape(blocks, groups, rows)
    scorer_labels = lax.dynamic_index_in_dim(every_label, scorer, 1, keepdims=False).reshape(-1)

    text_index = jnp.arange(blocks * rows, dtype=jnp.int32)
    hits = labels[:, None] == text_index[None, :]
    logits, hit_values, slopes = pair_slopes(images, all_texts, hits, temper, offset)
    total = jnp.sum(jax.nn.softplus(logits) - hit_values * logits)
    image_grads = temper * jnp.dot(slopes, all_texts, preferred_element_type=jnp.float32)

    own_index = blk_place * rows + jnp.arange(rows, dtype=jnp.int32)
    back_hits = own_index[:, None] == scorer_labels[None, :]
    back_slopes = pair_slopes(texts, all_images, back_hits, temper, offset)[2]
    text_grads = temper * jnp.dot(back_slopes, all_images, preferred_element_type=jnp.float32)

    total = lax.psum(total, ("blk", "group"))
    loss = total / (groups * rows * blocks * blocks)
    return (image_grads[None], text_grads[None], jnp.reshape(loss, (1,)))


def solution(mesh):
    in_specs = (P("group", "blk", None), P("group", "blk", None), P("group", "blk"), P(), P(), P())
    out_specs = (P("group", "blk", None), P("group", "blk", None), P())
    return jax.shard_map(shards, mesh=mesh, in_specs=in_specs, out_specs=out_specs, check_vma=False)
```

time: 174 us -> 134 us (0.77)
  waiting for transfers between devices: 61.8 us -> 0.04 us
  blocking collectives: 49.4 us -> 99.4 us
  matrix products: 24.4 us -> 8.29 us
  starting transfers between devices: 10.1 us -> 0.08 us
  loops' own time: 5.47 us -> 0 us
  between operations: 17.3 us -> 21.1 us
  local copies, waits for them, and re-layouts: 4.58 us -> 2.81 us
    ppermute x24 -> x0, waiting for transfers between devices: 61.7 us -> none  [shifted(): lax.ppermute(array, axis, [(i, (i + by) % size) for i in range(size)])]
    all_gather x1 -> x3, blocking collectives: 10.8 us -> 61.5 us  [the longest x1 41.4 us: shards(): lax.all_gather(labels, ('blk', 'group'), axis=0)]
    dot_general x24 -> x3, matrix products: 24.4 us -> 8.29 us  [the longest x1 4.02 us: shards(): jnp.dot(back_slopes, all_images, preferred_element_type=jnp.float32)]
    ppermute x24 -> x0, starting transfers between devices: 10 us -> none  [shifted(): lax.ppermute(array, axis, [(i, (i + by) % size) for i in range(size)])]
    another operation x1 -> x0, loops' own time: 5.47 us -> none  [shards(): finished = lax.fori_loop(0, cycle_size, advance, start)]
    unnamed x11 -> x10, local copies, waits for them, and re-layouts: 2.86 us -> 0.02 us
  transfers between devices with their start and end apart: 25 -> 2, of which waited for: 23 -> 0; matrix products, arithmetic and copies ran while one was open for 14% -> 4% of each run, Pallas kernels for 0% -> 0%
where the time goes in v1:
time: 134 us; the launch traced here: 132 us
  blocking collectives  99.4 us (74%)
  between operations  21.1 us (16%)
  matrix products  8.29 us (6%)
  local copies, waits for them, and re-layouts  2.81 us (2%)
    all_gather x1, blocking collectives, shards(): lax.all_gather(labels, ('blk', 'group'), axis=0)  41.4 us
    psum x1, blocking collectives, shards(): total = lax.psum(total, ('blk', 'group'))  37.9 us
    all_gather x1, blocking collectives, shards(): group_texts = lax.all_gather(texts, 'group', axis=0)  10.8 us
    all_gather x1, blocking collectives, shards(): group_images = lax.all_gather(images, 'group', axis=0)  9.26 us
    dot_general x1, matrix products, shards(): jnp.dot(back_slopes, all_images, preferred_element_type=jnp.float32)  4.02 us
    dot_general x1, matrix products, pair_slopes(): jnp.dot(rows, others.T, preferred_element_type=jnp.float32)  3 us
  transfers between devices with their start and end apart: 2, of which 0 were waited for; matrix products, arithmetic and copies ran while one was open for 4% of the time, Pallas kernels for 0%

profile of v1, /device:TPU:0, one launch (start us, length us, event | category | flops | bytes accessed | tf_op | source)
XLA Modules:
  0.0 132.4 jit_solution(14225385143605607776)
XLA Ops:
  7.2 0.0 copy-start.3
  7.2 0.0 copy-start
  7.2 0.0 all-gather.6.cloned.1.call-start
  7.2 1.3 dynamic_slice.14
  9.8 0.0 copy-start.2
  9.8 10.8 %all_gather.15 = bf16[4,96,1152]{2,1,0:T(8,128)(2,1)S(1)} all-gather(bf16[1,96,1152]{2,1,0:T(8,128)(2,1)} %param.7), channel_id=1, replica_groups=mesh['blk'=8,'group'=4] {'group'}, dimensions={0}, use_global_device_ids=true | all-gather | bytes 1105920 | tf_op jit(solution)/shard_map/all_gather | solution.py:28
  21.3 0.7 constant_dynamic-slice_fusion.1
  22.0 0.0 all-gather.6.cloned.1.call-update
  22.0 0.0 all-gather.8.cloned.1.call-start
  22.1 0.0 copy-done.3
  22.1 0.7 compare_reduce_fusion
  24.7 0.0 copy-done
  24.7 9.3 %all_gather.17 = bf16[4,96,1152]{2,1,0:T(8,128)(2,1)S(1)} all-gather(bf16[1,96,1152]{2,1,0:T(8,128)(2,1)S(1)} %copy-done), channel_id=1, replica_groups=mesh['blk'=8,'group'=4] {'group'}, dimensions={0}, use_global_device_ids=true | all-gather | bytes 1105920 | tf_op jit(solution)/shard_map/all_gather | solution.py:29
  33.9 0.7 constant_dynamic-slice_fusion
  34.6 0.0 all-gather.8.cloned.1.call-update
  36.0 0.0 copy-done.2
  36.0 41.4 %all-gather.2 = s32[32,1,96]{2,1,0:T(1,128)S(1)} all-gather(s32[1,1,96]{2,1,0:T(1,128)S(1)} %bitcast.71), channel_id=1, replica_groups=mesh['blk'=8,'group'=4] {'blk','group'}, dimensions={0}, use_global_device_ids=true | all-gather | bytes 12672 | tf_op jit(solution)/shard_map/all_gather | solution.py:34
  77.4 0.1 eq.45
  77.5 0.0 all-gather.6.cloned.1.call-done
  77.5 0.0 copy-start.4
  77.5 3.0 %fusion.47 = (f32[]{:T(128)}, f32[96,768]{1,0:T(8,128)S(1)}) fusion(s32[96]{0:T(128)S(1)} %bitcast.72, f32[]{:T(128)} %bitcast.68, bf16[1,96,1152]{2,1,0:T(8,128)(2,1)S(1)} %copy-done, bf16[1,768,1152]{2,1,0:T(8,128)(2,1)} %all-gather.6.cloned.1.call-done, f32[]{:T(128)} %bitcast), kind=kOutput, calls=%fused_computation.24 | convolution fusion | flops 170754048 | bytes 2285964 | tf_op jit(solution)/shard_map/dot_general | solution.py:8
  80.5 0.0 copy-start.1
  80.5 37.9 %psum.7 = f32[]{:T(128)} all-reduce(f32[]{:T(128)} %get-tuple-element.5), channel_id=1, replica_groups=mesh['blk'=8,'group'=4] {'blk','group'}, use_global_device_ids=true, to_apply=%region_2.3 | all-reduce | flops 1 | bytes 8 | tf_op jit(solution)/shard_map/psum | solution.py:48
  119.1 0.0 copy-done.4
  119.1 1.3 fusion
  120.4 0.0 all-gather.8.cloned.1.call-done
  120.4 0.0 copy-done.1
  120.4 4.0 %fusion.1 = f32[1,96,1152]{2,1,0:T(8,128)} fusion(bf16[1,768,1152]{2,1,0:T(8,128)(2,1)} %all-gather.8.cloned.1.call-done, bf16[1,96,1152]{2,1,0:T(8,128)(2,1)S(1)} %copy-done.1, f32[]{:T(128)} %bitcast, s32[768]{0:T(1024)S(1)} %eq.45, f32[]{:T(128)} %bitcast.69, s32[96]{0:T(128)S(1)} %iota_add_fusion), kind=kOutput, calls=%fused_computation.3 | convolution fusion | flops 340512768 | bytes 2436488 | tf_op jit(solution)/shard_map/dot_general | solution.py:46
  (2 shorter events, 0.0 us)
Async XLA Ops:
  7.2 14.9 %copy-start.3 = (s32[4]{0:T(128)S(1)}, s32[4]{0:T(128)}, u32[]{:S(2)}) copy-start(s32[4]{0:T(128)} %param.9) | copy-start | bytes 52
  7.2 17.5 %copy-start = (bf16[1,96,1152]{2,1,0:T(8,128)(2,1)S(1)}, bf16[1,96,1152]{2,1,0:T(8,128)(2,1)}, u32[]{:S(2)}) copy-start(bf16[1,96,1152]{2,1,0:T(8,128)(2,1)} %param.6) | copy-start | bytes 663556
  7.2 70.3 %all-gather.6.cloned.1.call-start = ((), (), s32[]{:S(2)}) async-start(), calls=%async_computation | async-start | bytes 1990656 | tf_op jit(solution)/shard_map/all_gather | solution.py:32
  9.8 26.2 %copy-start.2 = (s32[1,96]{1,0:T(1,128)S(1)}, s32[1,96]{1,0:T(1,128)}, u32[]{:S(2)}) copy-start(s32[1,96]{1,0:T(1,128)} %param.8) | copy-start | bytes 1156
  22.0 98.4 %all-gather.8.cloned.1.call-start = ((), (), s32[]{:S(2)}) async-start(), calls=%async_computation.1 | async-start | bytes 1990656 | tf_op jit(solution)/shard_map/all_gather | solution.py:33
  77.5 41.6 %copy-start.4 = (bf16[1,768,1152]{2,1,0:T(8,128)(2,1)S(1)}, bf16[1,768,1152]{2,1,0:T(8,128)(2,1)}, u32[]{:S(2)}) copy-start(bf16[1,768,1152]{2,1,0:T(8,128)(2,1)} %all-gather.6.cloned.1.call-done) | copy-start | bytes 5308420
  80.5 39.9 %copy-start.1 = (bf16[1,96,1152]{2,1,0:T(8,128)(2,1)S(1)}, bf16[1,96,1152]{2,1,0:T(8,128)(2,1)}, u32[]{:S(2)}) copy-start(bf16[1,96,1152]{2,1,0:T(8,128)(2,1)} %param.7) | copy-start | bytes 663556
Sparse Core Ops, SparseCore 0:
  22.1 46.8 all-gather.5
  71.2 45.0 all-gather.7
